TPU v7x, 32 devices: a whole 2x2x4 slice. The times are simulated.
32 devices in a mesh: region: 4 (over z), sub: 8 (over y, x, core).
Axes of the slice: x: 2, y: 2, z: 4, core: 2. Of those that a mesh axis runs over, the one named last changes fastest.
Arguments:
- test_vectors: float32 [16, 131072], P(None, ('region', 'sub')), may hold values from -12 to 12
- weights: bfloat16 [1024, 8, 128, 128], P(('region', 'sub')), may hold values from 0.099609375 to 1
- block_cols: int32 [1024, 8], P(('region', 'sub')), may hold values from 0 to 127, as said below
- block_count: int32 [1024], P(('region', 'sub')), may hold values from 5 to 8, as said below
- halo_send: int32 [32, 4, 16], P(('region', 'sub')), may hold values from 0 to 31
- far_send: int32 [32, 8, 4], P(('region', 'sub')), may hold values from 0 to 31
Outputs:
- smoothed: bfloat16 [16, 131072], P(None, ('region', 'sub'))
- affinity: bfloat16 [1024, 8, 128, 128], P(('region', 'sub'))
Inputs may be any that keep to these rules, and one draw needn't show every extreme that they name: `block_cols`: every table position is named by some live slot of its device's block rows. `block_count`: live slots of a block row come first.
All inputs are finite; a program needn't handle non-finite values.
Results may differ from a plain program's by a relative error of at most 0.0055.
Values may be sent and summed in bfloat16 or wider, within the bound.
A program may use at most 64 MiB of HBM per device.

v0:
```python
import jax
import jax.numpy as jnp
from jax import lax
from jax.sharding import PartitionSpec as P

SWEEPS = 3


damping = 2.0 / 3.0


def from_behind(block, axis, distance):
    devices = range(lax.axis_size(axis))
    route = [((i - distance) % len(devices), i) for i in devices]
    return lax.ppermute(block, axis, route)


def to_blocks(field, blk_count, blk_size):
    return field.reshape(field.shape[0], blk_count, blk_size).transpose(1, 0, 2)


def remote_blocks(blocks, halo_send, far_send):
    outgoing = blocks[halo_send[0]]
    far_out = blocks[far_send[0]]
    vec_count = blocks.shape[1]
    blk_size = blocks.shape[2]
    region_faces = []
    for direction, step_by in ((2, 1), (3, -1)):
        region_faces.append(from_behind(outgoing[direction], "region", step_by))
    sub_faces = []
    for direction, step_by in ((0, 1), (1, -1)):
        sub_faces.append(from_behind(outgoing[direction], "sub", step_by))
    far_in = lax.all_to_all(far_out, "sub", split_axis=0, concat_axis=0, tiled=True)
    far_flat = far_in.reshape(-1, vec_count, blk_size)
    return jnp.concatenate(sub_faces + region_faces + [far_flat], axis=0)


def local(test_vectors, weights, block_cols, block_count, halo_send, far_send):
    vec_count = test_vectors.shape[0]
    blk_count = weights.shape[0]
    slot_count = weights.shape[1]
    blk_size = weights.shape[2]
    zero_bf = jnp.zeros((), jnp.bfloat16)
    slot_ids = lax.broadcasted_iota(jnp.int32, (blk_count, slot_count), 1)
    valid_slot = slot_ids < block_count[:, None]
    live_wts = jnp.where(valid_slot[:, :, None, None], weights, zero_bf)
    degree = jnp.einsum(
        "rsab,b->ra",
        live_wts,
        jnp.ones((blk_size,), jnp.bfloat16),
        preferred_element_type=jnp.float32,
    )
    vectors = to_blocks(test_vectors, blk_count, blk_size)
    for sweep_index in range(SWEEPS):
        rounded = vectors.astype(jnp.bfloat16)
        block_table = jnp.concatenate(
            [rounded, remote_blocks(rounded, halo_send, far_send)], axis=0
        )
        applied = jnp.einsum(
            "rsab,rsvb->rva", live_wts, block_table[block_cols], preferred_element_type=jnp.float32
        )
        vectors = (1.0 - damping) * vectors + damping * applied / degree[:, None, :]
    norm_total = lax.psum(jnp.sum(vectors * vectors, axis=(0, 2)), ("region", "sub"))
    node_count = blk_count * blk_size * lax.axis_size("region") * lax.axis_size("sub")
    normal_vecs = (vectors / jnp.sqrt(norm_total / node_count)[None, :, None]).astype(jnp.bfloat16)
    block_table = jnp.concatenate(
        [normal_vecs, remote_blocks(normal_vecs, halo_send, far_send)], axis=0
    )
    gathered = block_table[block_cols]
    cross_terms = jnp.einsum(
        "rva,rsvb->rsab", normal_vecs, gathered, preferred_element_type=jnp.float32
    )
    own_float = normal_vecs.astype(jnp.float32)
    own_sq = jnp.sum(own_float * own_float, axis=1)
    far_float = gathered.astype(jnp.float32)
    far_sq = jnp.sum(far_float * far_float, axis=2)
    distance = (own_sq[:, None, :, None] + far_sq[:, :, None, :] - 2.0 * cross_terms) / vec_count
    affinity = (live_wts.astype(jnp.float32) / (1.0 + distance)).astype(jnp.bfloat16)
    smoothed = normal_vecs.transpose(1, 0, 2).reshape(vec_count, blk_count * blk_size)
    return (smoothed, affinity)


def solution(mesh):
    return jax.shard_map(
        local,
        mesh=mesh,
        in_specs=(
            P(None, ("region", "sub")),
            P(("region", "sub"), None, None, None),
            P(("region", "sub"), None),
            P(("region", "sub")),
            P(("region", "sub"), None, None),
            P(("region", "sub"), None, None),
        ),
        out_specs=(P(None, ("region", "sub")), P(("region", "sub"), None, None, None)),
        check_vma=False,
    )
```

profile of v0, /device:TPU:0, one launch (start us, length us, event | category | flops | bytes accessed | tf_op | source)
XLA Modules:
  0.0 162.8 jit_solution(1944018638875163099)
XLA Ops:
  0.6 0.7 compare_select_fusion.2
  1.3 0.1 reshape.111
  1.4 0.7 compare_select_fusion.1
  2.1 0.1 copy.37
  2.2 0.1 reshape.119
  2.3 1.1 multiply_bitcast_fusion
  3.4 1.2 gather_fusion.1
  4.6 5.2 %all-to-all-start = ((bf16[8,4,16,128]{3,2,1,0:T(8,128)(2,1)}), bf16[8,4,16,128]{3,2,1,0:T(8,128)(2,1)S(1)}, u32[]{:S(2)}, u32[]{:S(2)}) async-start(bf16[8,4,16,128]{3,2,1,0:T(8,128)(2,1)} %bitcast.3), calls=%async_computation | async-start | bytes 262144 | tf_op jit(solution)/shard_map/all_to_all | solution.py:33
  9.8 0.6 gather_fusion
  10.4 3.7 %collective-permute-start.3 = (bf16[16,16,128]{2,1,0:T(8,128)(2,1)S(1)}, bf16[16,16,128]{2,1,0:T(8,128)(2,1)S(1)}, u32[]{:S(2)}, u32[]{:S(2)}) collective-permute-start(bf16[16,16,128]{2,1,0:T(8,128)(2,1)S(1)} %get-tuple-element.31), channel_id=1, source_target_pairs={{8,0},{16,8},{24,16},{0,24},{9,1},{17,9},{25,17},{1,25},{10,2},{18... | collective-permute-start | bytes 196616 | tf_op jit(solution)/shard_map/ppermute | solution.py:15
  14.1 2.4 %collective-permute-start.1 = (bf16[16,16,128]{2,1,0:T(8,128)(2,1)S(1)}, bf16[16,16,128]{2,1,0:T(8,128)(2,1)S(1)}, u32[]{:S(2)}, u32[]{:S(2)}) collective-permute-start(bf16[16,16,128]{2,1,0:T(8,128)(2,1)S(1)} %get-tuple-element.33), channel_id=1, source_target_pairs={{1,0},{2,1},{3,2},{4,3},{5,4},{6,5},{7,6},{0,7},{9,8},{10,9},{11,1... | collective-permute-start | bytes 196616 | tf_op jit(solution)/shard_map/ppermute | solution.py:15
  16.5 0.0 collective-permute-start
  16.5 0.7 iota_compare_fusion
  17.3 0.7 compare_select_fusion
  18.0 0.1 copy.38
  18.0 0.1 reshape.127
  18.1 11.9 %copy.39 = bf16[32,8,128,128]{2,3,1,0:T(8,128)(2,1)} copy(bf16[32,8,128,128]{3,2,1,0:T(8,128)(2,1)} %param.7) | data formatting | bytes 16777216 | tf_op args[1]
  30.0 5.9 %convert_reduce_fusion = bf16[32,128,128]{1,2,0:T(8,128)(2,1)S(1)} fusion(bf16[32,8,128,128]{2,3,1,0:T(8,128)(2,1)} %copy.39, pred[32,8]{1,0:T(8,128)(4,1)S(1)} %iota_compare_fusion), kind=kLoop, calls=%fused_computation.13 | loop fusion | flops 12058624 | bytes 9437440 | tf_op jit(solution)/shard_map/rsab,b->ra/reduce_sum | solution.py:47
  35.9 0.2 fusion.28
  36.2 0.0 collective-permute-done
  36.2 0.0 collective-permute-done.1
  36.2 0.0 collective-permute-done.2
  36.3 0.0 all-to-all-done
  36.3 0.8 gather_fusion.2
  37.2 4.2 %constant_dynamic-update-slice_fusion.11 = (bf16[128,16,128]{2,1,0:T(8,128)(2,1)S(1)}, bf16[32,16,128]{2,1,0:T(8,128)(2,1)S(1)}, f32[32,16,128]{2,1,0:T(8,128)S(1)}, f32[32,16,128]{2,1,0:T(8,128)S(1)}) fusion(f32[2,32,8,128]{3,2,1,0:T(8,128)S(1)} %get-tuple-element.29, f32[32,128]{1,0:T(8,128)S(1)} %bitcast.138, bf16[32,8,16,128]{3,2,1,0:T(8,128)(2,1)S(1)} %bitcast.131, ...), kind=kOutput, calls=%fused_computation.67 | convolution fusion | flops 138674176 | bytes 10502400 | tf_op jit(solution)/shard_map/rsab,rsvb->rva/dot_general | solution.py:59
  41.4 0.6 gather_fusion.3
  42.1 0.1 collective-permute-start.4
  42.1 1.2 gather_fusion.4
  43.4 4.3 %all-to-all-start.1 = ((bf16[8,4,16,128]{3,2,1,0:T(8,128)(2,1)}), bf16[8,4,16,128]{3,2,1,0:T(8,128)(2,1)S(1)}, u32[]{:S(2)}, u32[]{:S(2)}) async-start(bf16[8,4,16,128]{3,2,1,0:T(8,128)(2,1)} %bitcast.12), calls=%async_computation.1 | async-start | bytes 262144 | tf_op jit(solution)/shard_map/all_to_all | solution.py:33
  47.7 3.5 %collective-permute-start.7 = (bf16[16,16,128]{2,1,0:T(8,128)(2,1)S(1)}, bf16[16,16,128]{2,1,0:T(8,128)(2,1)S(1)}, u32[]{:S(2)}, u32[]{:S(2)}) collective-permute-start(bf16[16,16,128]{2,1,0:T(8,128)(2,1)S(1)} %get-tuple-element.25), channel_id=1, source_target_pairs={{8,0},{16,8},{24,16},{0,24},{9,1},{17,9},{25,17},{1,25},{10,2},{18... | collective-permute-start | bytes 196616 | tf_op jit(solution)/shard_map/ppermute | solution.py:15
  51.2 0.0 collective-permute-start.6
  51.2 2.4 %collective-permute-start.5 = (bf16[16,16,128]{2,1,0:T(8,128)(2,1)S(1)}, bf16[16,16,128]{2,1,0:T(8,128)(2,1)S(1)}, u32[]{:S(2)}, u32[]{:S(2)}) collective-permute-start(bf16[16,16,128]{2,1,0:T(8,128)(2,1)S(1)} %get-tuple-element.27), channel_id=1, source_target_pairs={{1,0},{2,1},{3,2},{4,3},{5,4},{6,5},{7,6},{0,7},{9,8},{10,9},{11,1... | collective-permute-start | bytes 196616 | tf_op jit(solution)/shard_map/ppermute | solution.py:15
  53.6 0.0 collective-permute-done.4
  53.6 1.9 %collective-permute-done.5 = bf16[16,16,128]{2,1,0:T(8,128)(2,1)S(1)} collective-permute-done((bf16[16,16,128]{2,1,0:T(8,128)(2,1)S(1)}, bf16[16,16,128]{2,1,0:T(8,128)(2,1)S(1)}, u32[]{:S(2)}, u32[]{:S(2)}) %collective-permute-start.5) | collective-permute-done | bytes 65568 | tf_op jit(solution)/shard_map/ppermute | solution.py:15
  55.6 1.7 %collective-permute-done.6 = bf16[16,16,128]{2,1,0:T(8,128)(2,1)S(1)} collective-permute-done((bf16[16,16,128]{2,1,0:T(8,128)(2,1)S(1)}, bf16[16,16,128]{2,1,0:T(8,128)(2,1)S(1)}, u32[]{:S(2)}, u32[]{:S(2)}) %collective-permute-start.6) | collective-permute-done | bytes 65568 | tf_op jit(solution)/shard_map/ppermute | solution.py:15
  57.3 0.0 all-to-all-done.1
  57.4 0.8 gather_fusion.5
  58.2 4.2 %constant_dynamic-update-slice_fusion.17 = (bf16[128,16,128]{2,1,0:T(8,128)(2,1)S(1)}, bf16[32,16,128]{2,1,0:T(8,128)(2,1)S(1)}, f32[32,16,128]{2,1,0:T(8,128)S(1)}) fusion(f32[32,16,128]{2,1,0:T(8,128)S(1)} %get-tuple-element.16, f32[32,128]{1,0:T(8,128)S(1)} %bitcast.139, bf16[32,8,16,128]{3,2,1,0:T(8,128)(2,1)S(1)} %bitcast.133, ...), kind=kOutput, calls=%fused_computation.73 | convolution fusion | flops 138739712 | bytes 10240256 | tf_op jit(solution)/shard_map/rsab,rsvb->rva/dot_general | solution.py:59
  62.5 0.6 gather_fusion.6
  63.1 0.1 collective-permute-start.8
  63.2 1.2 gather_fusion.7
  64.4 4.5 %all-to-all-start.2 = ((bf16[8,4,16,128]{3,2,1,0:T(8,128)(2,1)}), bf16[8,4,16,128]{3,2,1,0:T(8,128)(2,1)S(1)}, u32[]{:S(2)}, u32[]{:S(2)}) async-start(bf16[8,4,16,128]{3,2,1,0:T(8,128)(2,1)} %bitcast.18), calls=%async_computation.2 | async-start | bytes 262144 | tf_op jit(solution)/shard_map/all_to_all | solution.py:33
  68.9 1.7 %collective-permute-start.11 = (bf16[16,16,128]{2,1,0:T(8,128)(2,1)S(1)}, bf16[16,16,128]{2,1,0:T(8,128)(2,1)S(1)}, u32[]{:S(2)}, u32[]{:S(2)}) collective-permute-start(bf16[16,16,128]{2,1,0:T(8,128)(2,1)S(1)} %get-tuple-element.21), channel_id=1, source_target_pairs={{8,0},{16,8},{24,16},{0,24},{9,1},{17,9},{25,17},{1,25},{10,2},{18... | collective-permute-start | bytes 196616 | tf_op jit(solution)/shard_map/ppermute | solution.py:15
  70.6 0.3 collective-permute-start.10
  70.9 2.1 %collective-permute-start.9 = (bf16[16,16,128]{2,1,0:T(8,128)(2,1)S(1)}, bf16[16,16,128]{2,1,0:T(8,128)(2,1)S(1)}, u32[]{:S(2)}, u32[]{:S(2)}) collective-permute-start(bf16[16,16,128]{2,1,0:T(8,128)(2,1)S(1)} %get-tuple-element.23), channel_id=1, source_target_pairs={{1,0},{2,1},{3,2},{4,3},{5,4},{6,5},{7,6},{0,7},{9,8},{10,9},{11,1... | collective-permute-start | bytes 196616 | tf_op jit(solution)/shard_map/ppermute | solution.py:15
  73.1 0.0 collective-permute-done.8
  73.1 1.9 %collective-permute-done.9 = bf16[16,16,128]{2,1,0:T(8,128)(2,1)S(1)} collective-permute-done((bf16[16,16,128]{2,1,0:T(8,128)(2,1)S(1)}, bf16[16,16,128]{2,1,0:T(8,128)(2,1)S(1)}, u32[]{:S(2)}, u32[]{:S(2)}) %collective-permute-start.9) | collective-permute-done | bytes 65568 | tf_op jit(solution)/shard_map/ppermute | solution.py:15
  75.0 1.7 %collective-permute-done.10 = bf16[16,16,128]{2,1,0:T(8,128)(2,1)S(1)} collective-permute-done((bf16[16,16,128]{2,1,0:T(8,128)(2,1)S(1)}, bf16[16,16,128]{2,1,0:T(8,128)(2,1)S(1)}, u32[]{:S(2)}, u32[]{:S(2)}) %collective-permute-start.10) | collective-permute-done | bytes 65568 | tf_op jit(solution)/shard_map/ppermute | solution.py:15
  76.7 0.8 gather_fusion.8
  77.6 4.4 %multiply_reduce_fusion.2 = (f32[16]{0:T(128)S(1)}, f32[32,16,128]{2,1,0:T(8,128)S(1)}) fusion(f32[32,16,128]{2,1,0:T(8,128)S(1)} %get-tuple-element.36, f32[32,16,128]{2,1,0:T(8,128)S(1)} %get-tuple-element.16, f32[32,128]{1,0:T(8,128)S(1)} %bitcast.140, bf16[32,8,16,128]{3,2,1,0:T(8,128)(2,1)S(1)} %bitcast.132, bf16[32,8,128,128]{2,3,1,0:T(8,128)(2,1)} %copy.39, ...), kind=kOutput, calls=%fused_computation.45 | convolution fusion | flops 138936304 | bytes 10240320 | tf_op jit(solution)/shard_map/rsab,rsvb->rva/dot_general | solution.py:59
  82.0 38.7 %psum.7 = f32[16]{0:T(128)S(1)} all-reduce(f32[16]{0:T(128)S(1)} %get-tuple-element.37), channel_id=1, replica_groups=mesh['region'=4,'sub'=8] {'region','sub'}, use_global_device_ids=true, to_apply=%region_2.3 | all-reduce | flops 16 | bytes 128 | tf_op jit(solution)/shard_map/psum | solution.py:63
  120.6 0.1 multiply_reduce_fusion.1
  120.8 1.2 gather_fusion.10
  122.0 0.6 gather_fusion.9
  122.7 0.7 copy_bitcast_fusion
  123.4 3.6 %all-to-all-start.3 = ((bf16[8,4,16,128]{3,2,1,0:T(8,128)(2,1)}), bf16[8,4,16,128]{3,2,1,0:T(8,128)(2,1)S(1)}, u32[]{:S(2)}, u32[]{:S(2)}) async-start(bf16[8,4,16,128]{3,2,1,0:T(8,128)(2,1)} %bitcast.24), calls=%async_computation.3 | async-start | bytes 262144 | tf_op jit(solution)/shard_map/all_to_all | solution.py:33
  127.0 2.0 %collective-permute-start.15 = (bf16[16,16,128]{2,1,0:T(8,128)(2,1)S(1)}, bf16[16,16,128]{2,1,0:T(8,128)(2,1)S(1)}, u32[]{:S(2)}, u32[]{:S(2)}) collective-permute-start(bf16[16,16,128]{2,1,0:T(8,128)(2,1)S(1)} %get-tuple-element.17), channel_id=1, source_target_pairs={{8,0},{16,8},{24,16},{0,24},{9,1},{17,9},{25,17},{1,25},{10,2},{18... | collective-permute-start | bytes 196616 | tf_op jit(solution)/shard_map/ppermute | solution.py:15
  129.0 0.7 collective-permute-start.14
  129.7 2.4 %collective-permute-start.13 = (bf16[16,16,128]{2,1,0:T(8,128)(2,1)S(1)}, bf16[16,16,128]{2,1,0:T(8,128)(2,1)S(1)}, u32[]{:S(2)}, u32[]{:S(2)}) collective-permute-start(bf16[16,16,128]{2,1,0:T(8,128)(2,1)S(1)} %get-tuple-element.19), channel_id=1, source_target_pairs={{1,0},{2,1},{3,2},{4,3},{5,4},{6,5},{7,6},{0,7},{9,8},{10,9},{11,1... | collective-permute-start | bytes 196616 | tf_op jit(solution)/shard_map/ppermute | solution.py:15
  132.1 4.6 %collective-permute-done.12 = bf16[16,16,128]{2,1,0:T(8,128)(2,1)S(1)} collective-permute-done((bf16[16,16,128]{2,1,0:T(8,128)(2,1)S(1)}, bf16[16,16,128]{2,1,0:T(8,128)(2,1)S(1)}, u32[]{:S(2)}, u32[]{:S(2)}) %collective-permute-start.12) | collective-permute-done | bytes 65568 | tf_op jit(solution)/shard_map/ppermute | solution.py:15
  136.8 0.8 gather_fusion.11
  137.6 0.4 multiply_reduce_fusion
  138.1 12.8 %fusion = bf16[32,8,128,128]{2,3,1,0:T(8,128)(2,1)} fusion(bf16[32,8,16,128]{3,2,1,0:T(8,128)(2,1)S(1)} %bitcast.128, f32[32,8,128]{2,1,0:T(8,128)S(1)} %multiply_reduce_fusion, f32[32,128]{1,0:T(8,128)S(1)} %get-tuple-element.10, bf16[32,8,128,128]{2,3,1,0:T(8,128)(2,1)} %copy.39, pred[32,8]{1,0:T(8,128)(4,1)S(1)} %iota_compare_fusion, ...), kind=kOutput, calls=%fused_computation.14 | convolution fusion | flops 171966464 | bytes 18104576 | tf_op jit(solution)/shard_map/rva,rsvb->rsab/dot_general | solution.py:70
  150.9 11.9 %copy.46 = bf16[32,8,128,128]{3,2,1,0:T(8,128)(2,1)} copy(bf16[32,8,128,128]{2,3,1,0:T(8,128)(2,1)} %fusion) | data formatting | bytes 16777216
  (40 shorter events, 0.5 us)
Async XLA Ops:
  4.6 31.7 %all-to-all-start = ((bf16[8,4,16,128]{3,2,1,0:T(8,128)(2,1)}), bf16[8,4,16,128]{3,2,1,0:T(8,128)(2,1)S(1)}, u32[]{:S(2)}, u32[]{:S(2)}) async-start(bf16[8,4,16,128]{3,2,1,0:T(8,128)(2,1)} %bitcast.3), calls=%async_computation | async-start | bytes 262144 | tf_op jit(solution)/shard_map/all_to_all | solution.py:33
  10.4 25.8 %collective-permute-start.3 = (bf16[16,16,128]{2,1,0:T(8,128)(2,1)S(1)}, bf16[16,16,128]{2,1,0:T(8,128)(2,1)S(1)}, u32[]{:S(2)}, u32[]{:S(2)}) collective-permute-start(bf16[16,16,128]{2,1,0:T(8,128)(2,1)S(1)} %get-tuple-element.31), channel_id=1, source_target_pairs={{8,0},{16,8},{24,16},{0,24},{9,1},{17,9},{25,17},{1,25},{10,2},{18... | collective-permute-start | bytes 196616 | tf_op jit(solution)/shard_map/ppermute | solution.py:15
  14.1 22.1 %collective-permute-start.2 = (bf16[16,16,128]{2,1,0:T(8,128)(2,1)S(1)}, bf16[16,16,128]{2,1,0:T(8,128)(2,1)S(1)}, u32[]{:S(2)}, u32[]{:S(2)}) collective-permute-start(bf16[16,16,128]{2,1,0:T(8,128)(2,1)S(1)} %get-tuple-element.32), channel_id=1, source_target_pairs={{24,0},{0,8},{8,16},{16,24},{25,1},{1,9},{9,17},{17,25},{26,2},{2,... | collective-permute-start | bytes 196616 | tf_op jit(solution)/shard_map/ppermute | solution.py:15
  14.1 22.1 %collective-permute-start.1 = (bf16[16,16,128]{2,1,0:T(8,128)(2,1)S(1)}, bf16[16,16,128]{2,1,0:T(8,128)(2,1)S(1)}, u32[]{:S(2)}, u32[]{:S(2)}) collective-permute-start(bf16[16,16,128]{2,1,0:T(8,128)(2,1)S(1)} %get-tuple-element.33), channel_id=1, source_target_pairs={{1,0},{2,1},{3,2},{4,3},{5,4},{6,5},{7,6},{0,7},{9,8},{10,9},{11,1... | collective-permute-start | bytes 196616 | tf_op jit(solution)/shard_map/ppermute | solution.py:15
  16.5 19.7 %collective-permute-start = (bf16[16,16,128]{2,1,0:T(8,128)(2,1)S(1)}, bf16[16,16,128]{2,1,0:T(8,128)(2,1)S(1)}, u32[]{:S(2)}, u32[]{:S(2)}) collective-permute-start(bf16[16,16,128]{2,1,0:T(8,128)(2,1)S(1)} %get-tuple-element.34), channel_id=1, source_target_pairs={{7,0},{0,1},{1,2},{2,3},{3,4},{4,5},{5,6},{6,7},{15,8},{8,9},{9,10... | collective-permute-start | bytes 196616 | tf_op jit(solution)/shard_map/ppermute | solution.py:15
  42.1 11.6 %collective-permute-start.4 = (bf16[16,16,128]{2,1,0:T(8,128)(2,1)S(1)}, bf16[16,16,128]{2,1,0:T(8,128)(2,1)S(1)}, u32[]{:S(2)}, u32[]{:S(2)}) collective-permute-start(bf16[16,16,128]{2,1,0:T(8,128)(2,1)S(1)} %get-tuple-element.28), channel_id=1, source_target_pairs={{7,0},{0,1},{1,2},{2,3},{3,4},{4,5},{5,6},{6,7},{15,8},{8,9},{9,10... | collective-permute-start | bytes 196616 | tf_op jit(solution)/shard_map/ppermute | solution.py:15
  43.4 14.0 %all-to-all-start.1 = ((bf16[8,4,16,128]{3,2,1,0:T(8,128)(2,1)}), bf16[8,4,16,128]{3,2,1,0:T(8,128)(2,1)S(1)}, u32[]{:S(2)}, u32[]{:S(2)}) async-start(bf16[8,4,16,128]{3,2,1,0:T(8,128)(2,1)} %bitcast.12), calls=%async_computation.1 | async-start | bytes 262144 | tf_op jit(solution)/shard_map/all_to_all | solution.py:33
  47.7 9.6 %collective-permute-start.7 = (bf16[16,16,128]{2,1,0:T(8,128)(2,1)S(1)}, bf16[16,16,128]{2,1,0:T(8,128)(2,1)S(1)}, u32[]{:S(2)}, u32[]{:S(2)}) collective-permute-start(bf16[16,16,128]{2,1,0:T(8,128)(2,1)S(1)} %get-tuple-element.25), channel_id=1, source_target_pairs={{8,0},{16,8},{24,16},{0,24},{9,1},{17,9},{25,17},{1,25},{10,2},{18... | collective-permute-start | bytes 196616 | tf_op jit(solution)/shard_map/ppermute | solution.py:15
  51.2 6.1 %collective-permute-start.6 = (bf16[16,16,128]{2,1,0:T(8,128)(2,1)S(1)}, bf16[16,16,128]{2,1,0:T(8,128)(2,1)S(1)}, u32[]{:S(2)}, u32[]{:S(2)}) collective-permute-start(bf16[16,16,128]{2,1,0:T(8,128)(2,1)S(1)} %get-tuple-element.26), channel_id=1, source_target_pairs={{24,0},{0,8},{8,16},{16,24},{25,1},{1,9},{9,17},{17,25},{26,2},{2,... | collective-permute-start | bytes 196616 | tf_op jit(solution)/shard_map/ppermute | solution.py:15
  51.2 4.3 %collective-permute-start.5 = (bf16[16,16,128]{2,1,0:T(8,128)(2,1)S(1)}, bf16[16,16,128]{2,1,0:T(8,128)(2,1)S(1)}, u32[]{:S(2)}, u32[]{:S(2)}) collective-permute-start(bf16[16,16,128]{2,1,0:T(8,128)(2,1)S(1)} %get-tuple-element.27), channel_id=1, source_target_pairs={{1,0},{2,1},{3,2},{4,3},{5,4},{6,5},{7,6},{0,7},{9,8},{10,9},{11,1... | collective-permute-start | bytes 196616 | tf_op jit(solution)/shard_map/ppermute | solution.py:15
  63.1 9.9 %collective-permute-start.8 = (bf16[16,16,128]{2,1,0:T(8,128)(2,1)S(1)}, bf16[16,16,128]{2,1,0:T(8,128)(2,1)S(1)}, u32[]{:S(2)}, u32[]{:S(2)}) collective-permute-start(bf16[16,16,128]{2,1,0:T(8,128)(2,1)S(1)} %get-tuple-element.24), channel_id=1, source_target_pairs={{7,0},{0,1},{1,2},{2,3},{3,4},{4,5},{5,6},{6,7},{15,8},{8,9},{9,10... | collective-permute-start | bytes 196616 | tf_op jit(solution)/shard_map/ppermute | solution.py:15
  64.4 12.3 %all-to-all-start.2 = ((bf16[8,4,16,128]{3,2,1,0:T(8,128)(2,1)}), bf16[8,4,16,128]{3,2,1,0:T(8,128)(2,1)S(1)}, u32[]{:S(2)}, u32[]{:S(2)}) async-start(bf16[8,4,16,128]{3,2,1,0:T(8,128)(2,1)} %bitcast.18), calls=%async_computation.2 | async-start | bytes 262144 | tf_op jit(solution)/shard_map/all_to_all | solution.py:33
  68.9 7.8 %collective-permute-start.11 = (bf16[16,16,128]{2,1,0:T(8,128)(2,1)S(1)}, bf16[16,16,128]{2,1,0:T(8,128)(2,1)S(1)}, u32[]{:S(2)}, u32[]{:S(2)}) collective-permute-start(bf16[16,16,128]{2,1,0:T(8,128)(2,1)S(1)} %get-tuple-element.21), channel_id=1, source_target_pairs={{8,0},{16,8},{24,16},{0,24},{9,1},{17,9},{25,17},{1,25},{10,2},{18... | collective-permute-start | bytes 196616 | tf_op jit(solution)/shard_map/ppermute | solution.py:15
  70.6 6.1 %collective-permute-start.10 = (bf16[16,16,128]{2,1,0:T(8,128)(2,1)S(1)}, bf16[16,16,128]{2,1,0:T(8,128)(2,1)S(1)}, u32[]{:S(2)}, u32[]{:S(2)}) collective-permute-start(bf16[16,16,128]{2,1,0:T(8,128)(2,1)S(1)} %get-tuple-element.22), channel_id=1, source_target_pairs={{24,0},{0,8},{8,16},{16,24},{25,1},{1,9},{9,17},{17,25},{26,2},{2,... | collective-permute-start | bytes 196616 | tf_op jit(solution)/shard_map/ppermute | solution.py:15
  70.9 4.0 %collective-permute-start.9 = (bf16[16,16,128]{2,1,0:T(8,128)(2,1)S(1)}, bf16[16,16,128]{2,1,0:T(8,128)(2,1)S(1)}, u32[]{:S(2)}, u32[]{:S(2)}) collective-permute-start(bf16[16,16,128]{2,1,0:T(8,128)(2,1)S(1)} %get-tuple-element.23), channel_id=1, source_target_pairs={{1,0},{2,1},{3,2},{4,3},{5,4},{6,5},{7,6},{0,7},{9,8},{10,9},{11,1... | collective-permute-start | bytes 196616 | tf_op jit(solution)/shard_map/ppermute | solution.py:15
  123.4 13.3 %all-to-all-start.3 = ((bf16[8,4,16,128]{3,2,1,0:T(8,128)(2,1)}), bf16[8,4,16,128]{3,2,1,0:T(8,128)(2,1)S(1)}, u32[]{:S(2)}, u32[]{:S(2)}) async-start(bf16[8,4,16,128]{3,2,1,0:T(8,128)(2,1)} %bitcast.24), calls=%async_computation.3 | async-start | bytes 262144 | tf_op jit(solution)/shard_map/all_to_all | solution.py:33
  127.0 9.7 %collective-permute-start.15 = (bf16[16,16,128]{2,1,0:T(8,128)(2,1)S(1)}, bf16[16,16,128]{2,1,0:T(8,128)(2,1)S(1)}, u32[]{:S(2)}, u32[]{:S(2)}) collective-permute-start(bf16[16,16,128]{2,1,0:T(8,128)(2,1)S(1)} %get-tuple-element.17), channel_id=1, source_target_pairs={{8,0},{16,8},{24,16},{0,24},{9,1},{17,9},{25,17},{1,25},{10,2},{18... | collective-permute-start | bytes 196616 | tf_op jit(solution)/shard_map/ppermute | solution.py:15
  129.0 7.7 %collective-permute-start.14 = (bf16[16,16,128]{2,1,0:T(8,128)(2,1)S(1)}, bf16[16,16,128]{2,1,0:T(8,128)(2,1)S(1)}, u32[]{:S(2)}, u32[]{:S(2)}) collective-permute-start(bf16[16,16,128]{2,1,0:T(8,128)(2,1)S(1)} %get-tuple-element.18), channel_id=1, source_target_pairs={{24,0},{0,8},{8,16},{16,24},{25,1},{1,9},{9,17},{17,25},{26,2},{2,... | collective-permute-start | bytes 196616 | tf_op jit(solution)/shard_map/ppermute | solution.py:15
  129.7 7.0 %collective-permute-start.13 = (bf16[16,16,128]{2,1,0:T(8,128)(2,1)S(1)}, bf16[16,16,128]{2,1,0:T(8,128)(2,1)S(1)}, u32[]{:S(2)}, u32[]{:S(2)}) collective-permute-start(bf16[16,16,128]{2,1,0:T(8,128)(2,1)S(1)} %get-tuple-element.19), channel_id=1, source_target_pairs={{1,0},{2,1},{3,2},{4,3},{5,4},{6,5},{7,6},{0,7},{9,8},{10,9},{11,1... | collective-permute-start | bytes 196616 | tf_op jit(solution)/shard_map/ppermute | solution.py:15
  132.0 4.6 %collective-permute-start.12 = (bf16[16,16,128]{2,1,0:T(8,128)(2,1)S(1)}, bf16[16,16,128]{2,1,0:T(8,128)(2,1)S(1)}, u32[]{:S(2)}, u32[]{:S(2)}) collective-permute-start(bf16[16,16,128]{2,1,0:T(8,128)(2,1)S(1)} %get-tuple-element.20), channel_id=1, source_target_pairs={{7,0},{0,1},{1,2},{2,3},{3,4},{4,5},{5,6},{6,7},{15,8},{8,9},{9,10... | collective-permute-start | bytes 196616 | tf_op jit(solution)/shard_map/ppermute | solution.py:15
where the time goes:
time: 164 us; the launch traced here: 163 us
  starting transfers between devices  38.8 us (24%)
  blocking collectives  38.7 us (24%)
  local copies, waits for them, and re-layouts  35.5 us (22%)
  matrix products  25.9 us (16%)
  waiting for transfers between devices  11.8 us (7%)
  other arithmetic  11.1 us (7%)
    psum x1, blocking collectives, local(): lax.psum(jnp.sum(vectors * vectors, axis=(0, 2)), ('region', 'sub'))  38.7 us
    unnamed x20, local copies, waits for them, and re-layouts  24.1 us
    ppermute x16, starting transfers between devices, from_behind(): return lax.ppermute(block, axis, route)  21.3 us
    all_to_all x4, starting transfers between devices, remote_blocks(): lax.all_to_all(far_out, 'sub', split_axis=0, concat_axis=0, tiled=True)  17.5 us
    dot_general x3, matrix products, local(): jnp.einsum('rsab,rsvb->rva', live_wts, block_table[block_cols], preferred...  12.8 us
    dot_general x1, matrix products, local(): jnp.einsum('rva,rsvb->rsab', normal_vecs, gathered, preferred_element_typ...  12.8 us
    ppermute x16, waiting for transfers between devices, from_behind(): return lax.ppermute(block, axis, route)  11.8 us
    reduce_sum x1, other arithmetic, local(): jnp.einsum('rsab,b->ra', live_wts, jnp.ones((blk_size,), jnp.bfloat16), p...  5.86 us
  transfers between devices with their start and end apart: 20, of which 5 were waited for; matrix products, arithmetic and copies ran while one was open for 14% of the time, Pallas kernels for 0%

commit v1 on v0

v1 whole, which is shorter than its diff:
```python
import functools

import jax
import jax.numpy as jnp
from jax import lax
from jax.experimental import pallas as pl
from jax.experimental.pallas import tpu as pltpu
from jax.sharding import PartitionSpec as P

SWEEPS = 3
MIN_LIVE = 5
EXTRA = 16

damping = 2.0 / 3.0

f32 = jnp.float32
bf16 = jnp.bfloat16
MESH = pl.DeviceIdType.MESH


def relax_kernel(
    n_region,
    n_sub,
    cols_ref,
    count_ref,
    halo_ref,
    far_ref,
    start_ref,
    weights_hbm,
    own_out,
    table_out,
    wts,
    vec,
    scale,
    own,
    marks,
    part_sub,
    part_region,
    *rest,
):
    tables, sends = rest[: SWEEPS + 1], rest[SWEEPS + 1 : 2 * SWEEPS + 2]
    wts_sem, send_sem, recv_sem, norm_send_sem, norm_recv_sem = rest[2 * SWEEPS + 2 :]
    rows, slots, size = wts.shape[:3]
    vecs = vec.shape[1]
    halo = halo_ref.shape[2]
    far = far_ref.shape[2]
    zero_at = tables[0].shape[0] - 1
    far_at = rows + 4 * halo
    me_sub, me_region = lax.axis_index("sub"), lax.axis_index("region")

    barrier = pltpu.get_barrier_semaphore()
    for axis, me, count in (("sub", me_sub, n_sub), ("region", me_region, n_region)):
        for j in range(1, count):
            pl.semaphore_signal(
                barrier, inc=1, device_id={axis: lax.rem(me + j, count)}, device_id_type=MESH
            )

    chunks = wts_sem.shape[0]
    per = rows // chunks
    loads = []
    for c in range(chunks):
        span = pl.ds(c * per, per)
        load = pltpu.make_async_copy(weights_hbm.at[span], wts.at[span], wts_sem.at[c])
        load.start()
        loads.append(load)

    marks[0] = jnp.ones((vecs, size), bf16)
    marks[1] = jnp.zeros((vecs, size), bf16)
    for table in tables:
        table[zero_at] = jnp.zeros((vecs, size), bf16)
    for r in range(rows):
        rounded = start_ref[:, r * size : (r + 1) * size].astype(bf16)
        own[r] = rounded
        tables[0][r] = rounded

    def exchange(k):
        table, send = tables[k], sends[k]
        copies = []
        faces = ((2, "region", me_region, n_region, 1), (3, "region", me_region, n_region, -1),
                 (0, "sub", me_sub, n_sub, 1), (1, "sub", me_sub, n_sub, -1))
        for face, axis, me, count, step in faces:
            def pick(i, carry):
                send[face * halo + i] = own[halo_ref[0, face, i]]
                return carry
            lax.fori_loop(0, halo, pick, 0, unroll=True)
            copy = pltpu.make_async_remote_copy(
                src_ref=send.at[pl.ds(face * halo, halo)],
                dst_ref=table.at[pl.ds(rows + face * halo, halo)],
                send_sem=send_sem.at[k, face],
                recv_sem=recv_sem.at[k, face],
                device_id={axis: lax.rem(me + step + count, count)},
                device_id_type=MESH,
            )
            copy.start()
            copies.append(copy)
        for j in range(1, n_sub):
            to = lax.rem(me_sub + j, n_sub)
            base = 4 * halo + (j - 1) * far
            for i in range(far):
                send[base + i] = own[far_ref[0, to, i]]
            copy = pltpu.make_async_remote_copy(
                src_ref=send.at[pl.ds(base, far)],
                dst_ref=table.at[pl.ds(far_at + me_sub * far, far)],
                send_sem=send_sem.at[k, 3 + j],
                recv_sem=recv_sem.at[k, 3 + j],
                device_id={"sub": to},
                device_id_type=MESH,
            )
            copy.start()
            copies.append(copy)
        for i in range(far):
            table[far_at + me_sub * far + i] = own[far_ref[0, me_sub, i]]
        return copies

    def sweep(k, first_row, row_count, total):
        table = tables[k]

        def one_row(r, total):
            live = [s < count_ref[r] for s in range(slots)]
            where = [jnp.where(live[s], cols_ref[r, s], zero_at) for s in range(slots)]
            left = jnp.concatenate([table[where[s]] for s in range(slots)], axis=1)
            if k == 0:
                ones = [marks[jnp.where(live[s], 0, 1)] for s in range(slots)]
                left = jnp.concatenate([left, jnp.concatenate(ones, axis=1)], axis=0)
            right = jnp.concatenate([wts[r, s] for s in range(slots)], axis=1)
            applied = lax.dot_general(
                left, right, (((1,), (1,)), ((), ())), preferred_element_type=f32
            )
            if k == 0:
                weight = damping / applied[vecs:]
                scale[r] = weight
                applied = applied[:vecs]
                held = start_ref[:, pl.ds(pl.multiple_of(r * size, size), size)]
            else:
                weight = scale[r]
                held = vec[r]
            moved = (1.0 - damping) * held + applied * weight
            vec[r] = moved
            rounded = moved.astype(bf16)
            own[r] = rounded
            if k + 1 < SWEEPS:
                tables[k + 1][r] = rounded
                return total
            return total + moved * moved

        return lax.fori_loop(first_row, first_row + row_count, one_row, total, unroll=2)

    pl.semaphore_wait(barrier, n_sub + n_region - 2)
    started = []
    total = jnp.zeros((vecs, size), f32)
    for k in range(SWEEPS):
        copies = exchange(k)
        started += copies
        for copy in copies:
            copy.wait_recv()
        if k == 0:
            for c in range(chunks):
                loads[c].wait()
                sweep(k, c * per, per, jnp.zeros((vecs, size), f32))
        else:
            total = sweep(k, 0, rows, jnp.zeros((vecs, size), f32))

    def share(part, value, axis, me, count, first_sem):
        part[me] = value
        copies = []
        for j in range(1, count):
            copy = pltpu.make_async_remote_copy(
                src_ref=part.at[me],
                dst_ref=part.at[me],
                send_sem=norm_send_sem.at[first_sem + j],
                recv_sem=norm_recv_sem.at[first_sem + j],
                device_id={axis: lax.rem(me + j, count)},
                device_id_type=MESH,
            )
            copy.start()
            copies.append(copy)
        return copies

    def added(part, copies):
        for copy in copies:
            copy.wait_recv()
        value = part[0]
        for q in range(1, part.shape[0]):
            value = value + part[q]
        return value

    norm_sub = share(part_sub, total, "sub", me_sub, n_sub, 0)
    copies = exchange(SWEEPS)
    started += copies
    sub_total = added(part_sub, norm_sub)
    norm_region = share(part_region, sub_total, "region", me_region, n_region, n_sub)
    full = added(part_region, norm_region)
    norm_total = jnp.sum(full, axis=1, keepdims=True)
    nodes = rows * size * n_region * n_sub
    factor = jnp.broadcast_to(1.0 / jnp.sqrt(norm_total / nodes), (vecs, size))
    row_id = lax.broadcasted_iota(jnp.int32, (EXTRA, size), 0)

    def pieces(value):
        top = value.astype(bf16).astype(f32)
        middle = (value - top).astype(bf16).astype(f32)
        return top, middle, value - top - middle

    def squares(values):
        held = values.astype(f32)
        return jnp.sum(held * held, axis=0, keepdims=True) * (1.0 / vecs)

    def far_form(values):
        top, middle, low = pieces(squares(values))
        extra = jnp.where(row_id == 0, top, jnp.where(row_id == 1, middle, jnp.where(
            row_id == 2, low, jnp.where(row_id < 6, 1.0, 0.0))))
        return extra.astype(bf16)

    def own_form(values):
        top, middle, low = pieces(squares(values) + 1.0)
        extra = jnp.where(row_id == 3, top, jnp.where(row_id == 4, middle, jnp.where(
            row_id == 5, low, jnp.where(row_id < 3, 1.0, 0.0))))
        return extra.astype(bf16)

    def own_row(r, carry):
        values = (vec[r] * factor).astype(bf16)
        own_out[r, 0:vecs] = values * (-2.0 / vecs)
        own_out[r, vecs : vecs + EXTRA] = own_form(values)
        table_out[r, 0:vecs] = values
        table_out[r, vecs : vecs + EXTRA] = far_form(values)
        return carry

    lax.fori_loop(0, rows, own_row, 0, unroll=2)
    for copy in copies:
        copy.wait_recv()

    def far_row(p, carry):
        values = (tables[SWEEPS][p].astype(f32) * factor).astype(bf16)
        table_out[p, 0:vecs] = values
        table_out[p, vecs : vecs + EXTRA] = far_form(values)
        return carry

    lax.fori_loop(rows, zero_at, far_row, 0, unroll=2)
    for copy in started + norm_sub + norm_region:
        copy.wait_send()


def affinity_kernel(cols_ref, count_ref, own_ref, table_ref, wts_ref, smoothed_ref, aff_ref):
    per, slots, size = wts_ref.shape[:3]
    vecs = smoothed_ref.shape[0]
    step = pl.program_id(0)

    for i in range(per):
        r = step * per + i
        near = own_ref[i]
        smoothed_ref[:, i * size : (i + 1) * size] = table_ref[r, 0:vecs]
        far = jnp.concatenate([table_ref[cols_ref[r, s]] for s in range(slots)], axis=1)
        below = lax.dot_general(
            near, far, (((0,), (0,)), ((), ())), preferred_element_type=f32
        )
        for s in range(slots):
            ratio = pl.reciprocal(below[:, s * size : (s + 1) * size], approx=True)
            value = wts_ref[i, s].astype(f32) * ratio
            if s >= MIN_LIVE:
                value = jnp.where(s < count_ref[r], value, 0.0)
            aff_ref[i, s] = value.astype(bf16)


def local(n_region, n_sub, test_vectors, weights, block_cols, block_count, halo_send, far_send):
    vecs = test_vectors.shape[0]
    rows, slots, size, _ = weights.shape
    halo, far = halo_send.shape[2], far_send.shape[2]
    table = rows + 4 * halo + n_sub * far
    block = (vecs, size)
    smem = pl.BlockSpec(memory_space=pltpu.SMEM)
    vmem = pl.BlockSpec(memory_space=pltpu.VMEM)
    chunks = 8
    own_blocks, table_blocks = pl.pallas_call(
        functools.partial(relax_kernel, n_region, n_sub),
        out_shape=(
            jax.ShapeDtypeStruct((rows, vecs + EXTRA, size), bf16),
            jax.ShapeDtypeStruct((table, vecs + EXTRA, size), bf16),
        ),
        in_specs=[smem, smem, smem, smem, vmem, pl.BlockSpec(memory_space=pl.ANY)],
        out_specs=(vmem, vmem),
        scratch_shapes=[
            pltpu.VMEM(weights.shape, bf16),
            pltpu.VMEM((rows,) + block, f32),
            pltpu.VMEM((rows,) + block, f32),
            pltpu.VMEM((rows,) + block, bf16),
            pltpu.VMEM((2,) + block, bf16),
            pltpu.VMEM((n_sub,) + block, f32),
            pltpu.VMEM((n_region,) + block, f32),
        ]
        + [pltpu.VMEM((table + 1,) + block, bf16)] * (SWEEPS + 1)
        + [pltpu.VMEM((4 * halo + (n_sub - 1) * far,) + block, bf16)] * (SWEEPS + 1)
        + [
            pltpu.SemaphoreType.DMA((chunks,)),
            pltpu.SemaphoreType.DMA((SWEEPS + 1, 3 + n_sub)),
            pltpu.SemaphoreType.DMA((SWEEPS + 1, 3 + n_sub)),
            pltpu.SemaphoreType.DMA((n_sub + n_region,)),
            pltpu.SemaphoreType.DMA((n_sub + n_region,)),
        ],
        compiler_params=pltpu.CompilerParams(
            collective_id=0, has_side_effects=True, vmem_limit_bytes=40 * 1024 * 1024
        ),
        name="relax",
    )(block_cols, block_count, halo_send, far_send, test_vectors, weights)

    per = 4
    smoothed, affinity = pl.pallas_call(
        affinity_kernel,
        out_shape=(
            jax.ShapeDtypeStruct((vecs, rows * size), bf16),
            jax.ShapeDtypeStruct(weights.shape, bf16),
        ),
        grid=(rows // per,),
        in_specs=[
            smem,
            smem,
            pl.BlockSpec((per, vecs + EXTRA, size), lambda i: (i, 0, 0)),
            pl.BlockSpec((table, vecs + EXTRA, size), lambda i: (0, 0, 0)),
            pl.BlockSpec((per, slots, size, size), lambda i: (i, 0, 0, 0)),
        ],
        out_specs=(
            pl.BlockSpec((vecs, per * size), lambda i: (0, i)),
            pl.BlockSpec((per, slots, size, size), lambda i: (i, 0, 0, 0)),
        ),
        compiler_params=pltpu.CompilerParams(vmem_limit_bytes=32 * 1024 * 1024),
        name="affinity",
    )(block_cols, block_count, own_blocks, table_blocks, weights)
    return smoothed, affinity


def solution(mesh):
    return jax.shard_map(
        functools.partial(local, mesh.shape["region"], mesh.shape["sub"]),
        mesh=mesh,
        in_specs=(
            P(None, ("region", "sub")),
            P(("region", "sub"), None, None, None),
            P(("region", "sub"), None),
            P(("region", "sub")),
            P(("region", "sub"), None, None),
            P(("region", "sub"), None, None),
        ),
        out_specs=(P(None, ("region", "sub")), P(("region", "sub"), None, None, None)),
        check_vma=False,
    )
```

time: 164 us -> 60.1 us (0.37)
  Pallas kernels: 0 us -> 52 us
  starting transfers between devices: 38.8 us -> 0 us
  blocking collectives: 38.7 us -> 0 us
  local copies, waits for them, and re-layouts: 35.5 us -> 7.19 us
  matrix products: 25.9 us -> 0 us
  waiting for transfers between devices: 11.8 us -> 0 us
  other arithmetic: 11.1 us -> 0 us
    pallas_call x0 -> x2, Pallas kernels: none -> 52 us  [the longest x1 44.8 us: local(): pl.pallas_call(functools.partial(relax_kernel, n_region, n_sub), out_shap...]
    psum x1 -> x0, blocking collectives: 38.7 us -> none  [local(): lax.psum(jnp.sum(vectors * vectors, axis=(0, 2)), ('region', 'sub'))]
    dot_general x5 -> x0, matrix products: 25.9 us -> none  [the longest x3 12.8 us: local(): jnp.einsum('rsab,rsvb->rva', live_wts, block_table[block_cols], preferred...]
    ppermute x16 -> x0, starting transfers between devices: 21.3 us -> none  [from_behind(): return lax.ppermute(block, axis, route)]
    all_to_all x4 -> x0, starting transfers between devices: 17.5 us -> none  [remote_blocks(): lax.all_to_all(far_out, 'sub', split_axis=0, concat_axis=0, tiled=True)]
    unnamed x20 -> x12, local copies, waits for them, and re-layouts: 24.1 us -> 7.19 us
    ppermute x16 -> x0, waiting for transfers between devices: 11.8 us -> none  [from_behind(): return lax.ppermute(block, axis, route)]
    gather x12 -> x0, local copies, waits for them, and re-layouts: 10.9 us -> none  [the longest x4 4.95 us: remote_blocks(): far_out = blocks[far_send[0]]]
  transfers between devices with their start and end apart: 20 -> 0, of which waited for: 5 -> 0; matrix products, arithmetic and copies ran while one was open for 14% -> 0% of each run, Pallas kernels for 0% -> 0%
where the time goes in v1:
time: 60.1 us; the launch traced here: 59.8 us
  Pallas kernels  52 us (87%)
  local copies, waits for them, and re-layouts  7.19 us (12%)
  between operations  0.65 us (1%)
    pallas_call x1, Pallas kernels, local(): pl.pallas_call(functools.partial(relax_kernel, n_region, n_sub), out_shap...  44.8 us
    unnamed x12, local copies, waits for them, and re-layouts  7.19 us
    pallas_call x1, Pallas kernels, local(): pl.pallas_call(affinity_kernel, out_shape=(jax.ShapeDtypeStruct((vecs, ro...  7.15 us

profile of v1, /device:TPU:0, one launch (start us, length us, event | category | flops | bytes accessed | tf_op | source)
XLA Modules:
  0.0 59.8 jit_solution(15048965054940020243)
XLA Ops:
  0.6 0.8 %copy.9.far_ref = s32[1,8,4]{2,1,0:T(8,128)S(1)} copy(s32[1,8,4]{1,2,0:T(4,128)} %param.11) | data formatting | bytes 256 | tf_op args[5]
  1.4 0.8 %copy.10.cols_ref = s32[32,8]{1,0:T(8,128)S(1)} copy(s32[32,8]{0,1:T(8,128)} %param.8) | data formatting | bytes 2048 | tf_op args[2]
  2.1 0.0 copy-start
  2.1 3.4 %copy-done = bf16[32,8,128,128]{3,2,1,0:T(8,128)(2,1)S(1)} copy-done((bf16[32,8,128,128]{3,2,1,0:T(8,128)(2,1)S(1)}, bf16[32,8,128,128]{3,2,1,0:T(8,128)(2,1)}, u32[]{:S(2)}) %copy-start) | copy-done | bytes 8388632
  5.5 0.0 copy-start.2
  5.5 0.9 %copy-done.2 = f32[16,4096]{1,0:T(8,128)S(1)} copy-done((f32[16,4096]{1,0:T(8,128)S(1)}, f32[16,4096]{1,0:T(8,128)}, u32[]{:S(2)}) %copy-start.2) | copy-done | bytes 262168
  6.5 0.0 copy-start.3
  6.5 0.7 %copy-done.3 = s32[1,4,16]{2,1,0:T(4,128)S(1)} copy-done((s32[1,4,16]{2,1,0:T(4,128)S(1)}, s32[1,4,16]{2,1,0:T(4,128)}, u32[]{:S(2)}) %copy-start.3) | copy-done | bytes 280
  7.2 0.0 copy-start.4
  7.2 0.7 %copy-done.4 = s32[32]{0:T(128)S(1)} copy-done((s32[32]{0:T(128)S(1)}, s32[32]{0:T(128)}, u32[]{:S(2)}) %copy-start.4) | copy-done | bytes 152
  7.8 0.0 copy-start.1
  7.8 44.8 %relax.1 = (bf16[32,32,128]{2,1,0:T(8,128)(2,1)S(1)}, bf16[128,32,128]{2,1,0:T(8,128)(2,1)S(1)}) custom-call(s32[32,8]{1,0:T(8,128)S(1)} %copy.10.cols_ref, s32[32]{0:T(128)S(1)} %copy-done.4, s32[1,4,16]{2,1,0:T(4,128)S(1)} %copy-done.3, s32[1,8,4]{2,1,0:T(8,128)S(1)} %copy.9.far_ref, f32[16,4096]{1,0:T(8,128)S(1)} %copy-done.2, ...), custom_call_target="tpu_custom_call" | custom-call | tf_op jit(solution)/shard_map/relax/pallas_call | solution.py:272
  52.7 0.0 copy-done.1
  52.7 7.1 %affinity.1 = (bf16[16,4096]{1,0:T(8,128)(2,1)}, bf16[32,8,128,128]{3,2,1,0:T(8,128)(2,1)}) custom-call(s32[32,8]{1,0:T(8,128)S(1)} %copy.10.cols_ref, s32[32]{0:T(128)S(1)} %copy-done.4, bf16[32,32,128]{2,1,0:T(8,128)(2,1)S(1)} %get-tuple-element.4.own_ref, bf16[128,32,128]{2,1,0:T(8,128)(2,1)S(1)} %get-tuple-element.5.table_ref, ...), custom_call_target="tpu_custom_call" | custom-call | tf_op jit(solution)/shard_map/affinity/pallas_call | solution.py:305
Async XLA Ops:
  2.1 3.4 %copy-start = (bf16[32,8,128,128]{3,2,1,0:T(8,128)(2,1)S(1)}, bf16[32,8,128,128]{3,2,1,0:T(8,128)(2,1)}, u32[]{:S(2)}) copy-start(bf16[32,8,128,128]{3,2,1,0:T(8,128)(2,1)} %wts_ref.1) | copy-start | bytes 25165828
  5.5 0.9 %copy-start.2 = (f32[16,4096]{1,0:T(8,128)S(1)}, f32[16,4096]{1,0:T(8,128)}, u32[]{:S(2)}) copy-start(f32[16,4096]{1,0:T(8,128)} %start_ref.1) | copy-start | bytes 786436
  6.5 0.7 %copy-start.3 = (s32[1,4,16]{2,1,0:T(4,128)S(1)}, s32[1,4,16]{2,1,0:T(4,128)}, u32[]{:S(2)}) copy-start(s32[1,4,16]{2,1,0:T(4,128)} %halo_ref.1) | copy-start | bytes 772
  7.2 0.7 %copy-start.4 = (s32[32]{0:T(128)S(1)}, s32[32]{0:T(128)}, u32[]{:S(2)}) copy-start(s32[32]{0:T(128)} %count_ref.3) | copy-start | bytes 388
  7.8 44.8 %copy-start.1 = (bf16[32,8,128,128]{3,2,1,0:T(8,128)(2,1)S(1)}, bf16[32,8,128,128]{3,2,1,0:T(8,128)(2,1)}, u32[]{:S(2)}) copy-start(bf16[32,8,128,128]{3,2,1,0:T(8,128)(2,1)} %wts_ref.1) | copy-start | bytes 25165828

commit v2 on v1

--- a/solution.py
+++ b/solution.py
@@ -21,15 +21,21 @@
 def relax_kernel(
     n_region,
     n_sub,
+    cols_hbm,
+    count_hbm,
+    halo_hbm,
+    far_hbm,
+    start_hbm,
+    weights_hbm,
+    own_out,
+    table_out,
     cols_ref,
     count_ref,
     halo_ref,
     far_ref,
     start_ref,
-    weights_hbm,
-    own_out,
-    table_out,
     wts,
+    turned,
     vec,
     scale,
     own,
@@ -39,11 +45,11 @@
     *rest,
 ):
     tables, sends = rest[: SWEEPS + 1], rest[SWEEPS + 1 : 2 * SWEEPS + 2]
-    wts_sem, send_sem, recv_sem, norm_send_sem, norm_recv_sem = rest[2 * SWEEPS + 2 :]
+    list_sem, wts_sem, send_sem, recv_sem, norm_send_sem, norm_recv_sem = rest[2 * SWEEPS + 2 :]
     rows, slots, size = wts.shape[:3]
     vecs = vec.shape[1]
     halo = halo_ref.shape[2]
-    far = far_ref.shape[2]
+    far = far_ref.shape[1]
     zero_at = tables[0].shape[0] - 1
     far_at = rows + 4 * halo
     me_sub, me_region = lax.axis_index("sub"), lax.axis_index("region")
@@ -55,6 +61,14 @@
                 barrier, inc=1, device_id={axis: lax.rem(me + j, count)}, device_id_type=MESH
             )
 
+    small = ((start_hbm, start_ref), (halo_hbm, halo_ref), (far_hbm, far_ref),
+             (cols_hbm, cols_ref), (count_hbm, count_ref))
+    lists = [
+        pltpu.make_async_copy(source, target, list_sem.at[i])
+        for i, (source, target) in enumerate(small)
+    ]
+    for load in lists:
+        load.start()
     chunks = wts_sem.shape[0]
     per = rows // chunks
     loads = []
@@ -68,6 +82,7 @@
     marks[1] = jnp.zeros((vecs, size), bf16)
     for table in tables:
         table[zero_at] = jnp.zeros((vecs, size), bf16)
+    lists[0].wait()
     for r in range(rows):
         rounded = start_ref[:, r * size : (r + 1) * size].astype(bf16)
         own[r] = rounded
@@ -97,7 +112,7 @@
             to = lax.rem(me_sub + j, n_sub)
             base = 4 * halo + (j - 1) * far
             for i in range(far):
-                send[base + i] = own[far_ref[0, to, i]]
+                send[base + i] = own[far_ref[0, i, to]]
             copy = pltpu.make_async_remote_copy(
                 src_ref=send.at[pl.ds(base, far)],
                 dst_ref=table.at[pl.ds(far_at + me_sub * far, far)],
@@ -109,32 +124,37 @@
             copy.start()
             copies.append(copy)
         for i in range(far):
-            table[far_at + me_sub * far + i] = own[far_ref[0, me_sub, i]]
+            table[far_at + me_sub * far + i] = own[far_ref[0, i, me_sub]]
         return copies
 
-    def sweep(k, first_row, row_count, total):
+    def turn(r, carry):
+        ones = [marks[jnp.where(s < count_ref[r], 0, 1)] for s in range(slots)]
+        columns = jnp.concatenate([wts[r, s].T for s in range(slots)], axis=0)
+        turned[r] = columns
+        degree = lax.dot_general(
+            jnp.concatenate(ones, axis=1),
+            columns,
+            (((1,), (0,)), ((), ())),
+            preferred_element_type=f32,
+        )
+        scale[r] = damping / degree
+        return carry
+
+    def sweep(k, total):
         table = tables[k]
 
         def one_row(r, total):
             live = [s < count_ref[r] for s in range(slots)]
-            where = [jnp.where(live[s], cols_ref[r, s], zero_at) for s in range(slots)]
+            where = [jnp.where(live[s], cols_ref[s, r], zero_at) for s in range(slots)]
             left = jnp.concatenate([table[where[s]] for s in range(slots)], axis=1)
+            applied = lax.dot_general(
+                left, turned[r], (((1,), (0,)), ((), ())), preferred_element_type=f32
+            )
             if k == 0:
-                ones = [marks[jnp.where(live[s], 0, 1)] for s in range(slots)]
-                left = jnp.concatenate([left, jnp.concatenate(ones, axis=1)], axis=0)
-            right = jnp.concatenate([wts[r, s] for s in range(slots)], axis=1)
-            applied = lax.dot_general(
-                left, right, (((1,), (1,)), ((), ())), preferred_element_type=f32
-            )
-            if k == 0:
-                weight = damping / applied[vecs:]
-                scale[r] = weight
-                applied = applied[:vecs]
                 held = start_ref[:, pl.ds(pl.multiple_of(r * size, size), size)]
             else:
-                weight = scale[r]
                 held = vec[r]
-            moved = (1.0 - damping) * held + applied * weight
+            moved = (1.0 - damping) * held + applied * scale[r]
             vec[r] = moved
             rounded = moved.astype(bf16)
             own[r] = rounded
@@ -143,22 +163,23 @@
                 return total
             return total + moved * moved
 
-        return lax.fori_loop(first_row, first_row + row_count, one_row, total, unroll=2)
-
+        return lax.fori_loop(0, rows, one_row, total, unroll=8)
+
+    for load in lists[1:]:
+        load.wait()
     pl.semaphore_wait(barrier, n_sub + n_region - 2)
     started = []
     total = jnp.zeros((vecs, size), f32)
     for k in range(SWEEPS):
         copies = exchange(k)
         started += copies
-        for copy in copies:
-            copy.wait_recv()
         if k == 0:
             for c in range(chunks):
                 loads[c].wait()
-                sweep(k, c * per, per, jnp.zeros((vecs, size), f32))
-        else:
-            total = sweep(k, 0, rows, jnp.zeros((vecs, size), f32))
+                lax.fori_loop(c * per, (c + 1) * per, turn, 0, unroll=True)
+        for copy in copies:
+            copy.wait_recv()
+        total = sweep(k, jnp.zeros((vecs, size), f32))
 
     def share(part, value, axis, me, count, first_sem):
         part[me] = value
@@ -224,7 +245,7 @@
         table_out[r, vecs : vecs + EXTRA] = far_form(values)
         return carry
 
-    lax.fori_loop(0, rows, own_row, 0, unroll=2)
+    lax.fori_loop(0, rows, own_row, 0, unroll=4)
     for copy in copies:
         copy.wait_recv()
 
@@ -234,27 +255,27 @@
         table_out[p, vecs : vecs + EXTRA] = far_form(values)
         return carry
 
-    lax.fori_loop(rows, zero_at, far_row, 0, unroll=2)
+    lax.fori_loop(rows, zero_at, far_row, 0, unroll=8)
     for copy in started + norm_sub + norm_region:
         copy.wait_send()
 
 
 def affinity_kernel(cols_ref, count_ref, own_ref, table_ref, wts_ref, smoothed_ref, aff_ref):
-    per, slots, size = wts_ref.shape[:3]
+    per, slots, size = aff_ref.shape[:3]
     vecs = smoothed_ref.shape[0]
     step = pl.program_id(0)
 
     for i in range(per):
         r = step * per + i
-        near = own_ref[i]
+        near = own_ref[r]
         smoothed_ref[:, i * size : (i + 1) * size] = table_ref[r, 0:vecs]
-        far = jnp.concatenate([table_ref[cols_ref[r, s]] for s in range(slots)], axis=1)
+        far = jnp.concatenate([table_ref[cols_ref[s, r]] for s in range(slots)], axis=1)
         below = lax.dot_general(
             near, far, (((0,), (0,)), ((), ())), preferred_element_type=f32
         )
         for s in range(slots):
             ratio = pl.reciprocal(below[:, s * size : (s + 1) * size], approx=True)
-            value = wts_ref[i, s].astype(f32) * ratio
+            value = wts_ref[r, s].astype(f32) * ratio
             if s >= MIN_LIVE:
                 value = jnp.where(s < count_ref[r], value, 0.0)
             aff_ref[i, s] = value.astype(bf16)
@@ -269,16 +290,24 @@
     smem = pl.BlockSpec(memory_space=pltpu.SMEM)
     vmem = pl.BlockSpec(memory_space=pltpu.VMEM)
     chunks = 8
+    cols = block_cols.T
+    far_lists = far_send.transpose(0, 2, 1)
     own_blocks, table_blocks = pl.pallas_call(
         functools.partial(relax_kernel, n_region, n_sub),
         out_shape=(
             jax.ShapeDtypeStruct((rows, vecs + EXTRA, size), bf16),
             jax.ShapeDtypeStruct((table, vecs + EXTRA, size), bf16),
         ),
-        in_specs=[smem, smem, smem, smem, vmem, pl.BlockSpec(memory_space=pl.ANY)],
+        in_specs=[pl.BlockSpec(memory_space=pltpu.HBM)] * 6,
         out_specs=(vmem, vmem),
         scratch_shapes=[
+            pltpu.SMEM(cols.shape, jnp.int32),
+            pltpu.SMEM(block_count.shape, jnp.int32),
+            pltpu.SMEM(halo_send.shape, jnp.int32),
+            pltpu.SMEM(far_lists.shape, jnp.int32),
+            pltpu.VMEM(test_vectors.shape, f32),
             pltpu.VMEM(weights.shape, bf16),
+            pltpu.VMEM((rows, slots * size, size), bf16),
             pltpu.VMEM((rows,) + block, f32),
             pltpu.VMEM((rows,) + block, f32),
             pltpu.VMEM((rows,) + block, bf16),
@@ -289,6 +318,7 @@
         + [pltpu.VMEM((table + 1,) + block, bf16)] * (SWEEPS + 1)
         + [pltpu.VMEM((4 * halo + (n_sub - 1) * far,) + block, bf16)] * (SWEEPS + 1)
         + [
+            pltpu.SemaphoreType.DMA((5,)),
             pltpu.SemaphoreType.DMA((chunks,)),
             pltpu.SemaphoreType.DMA((SWEEPS + 1, 3 + n_sub)),
             pltpu.SemaphoreType.DMA((SWEEPS + 1, 3 + n_sub)),
@@ -299,7 +329,7 @@
             collective_id=0, has_side_effects=True, vmem_limit_bytes=40 * 1024 * 1024
         ),
         name="relax",
-    )(block_cols, block_count, halo_send, far_send, test_vectors, weights)
+    )(*[pltpu.with_memory_space_constraint(x, pltpu.HBM) for x in (cols, block_count, halo_send, far_lists, test_vectors, weights)])
 
     per = 4
     smoothed, affinity = pl.pallas_call(
@@ -312,9 +342,9 @@
         in_specs=[
             smem,
             smem,
-            pl.BlockSpec((per, vecs + EXTRA, size), lambda i: (i, 0, 0)),
-            pl.BlockSpec((table, vecs + EXTRA, size), lambda i: (0, 0, 0)),
-            pl.BlockSpec((per, slots, size, size), lambda i: (i, 0, 0, 0)),
+            vmem,
+            vmem,
+            vmem,
         ],
         out_specs=(
             pl.BlockSpec((vecs, per * size), lambda i: (0, i)),
@@ -322,7 +352,7 @@
         ),
         compiler_params=pltpu.CompilerParams(vmem_limit_bytes=32 * 1024 * 1024),
         name="affinity",
-    )(block_cols, block_count, own_blocks, table_blocks, weights)
+    )(cols, block_count, own_blocks, table_blocks, weights)
     return smoothed, affinity
 
 

time: 60.1 us -> 43 us (0.72)
  Pallas kernels: 52 us -> 42.1 us
  local copies, waits for them, and re-layouts: 7.19 us -> 0.01 us
    pallas_call x1, Pallas kernels: 44.8 us -> 35.2 us  [local(): pl.pallas_call(functools.partial(relax_kernel, n_region, n_sub), out_shap...]
    unnamed x12 -> x6, local copies, waits for them, and re-layouts: 7.19 us -> 0.01 us
where the time goes in v2:
time: 43 us; the launch traced here: 42.8 us
  Pallas kernels  42.1 us (98%)
  between operations  0.69 us (2%)
    pallas_call x1, Pallas kernels, local(): pl.pallas_call(functools.partial(relax_kernel, n_region, n_sub), out_shap...  35.2 us
    pallas_call x1, Pallas kernels, local(): pl.pallas_call(affinity_kernel, out_shape=(jax.ShapeDtypeStruct((vecs, ro...  6.95 us

profile of v2, /device:TPU:0, one launch (start us, length us, event | category | flops | bytes accessed | tf_op | source)
XLA Modules:
  0.0 42.8 jit_solution(13910294793655279433)
XLA Ops:
  0.6 0.0 copy-start.2
  0.6 0.0 copy-start
  0.7 0.0 copy-start.1
  0.7 35.2 %relax.1 = (bf16[32,32,128]{2,1,0:T(8,128)(2,1)S(1)}, bf16[128,32,128]{2,1,0:T(8,128)(2,1)S(1)}) custom-call(s32[8,32]{1,0:T(8,128)} %bitcast.2, s32[32]{0:T(128)} %count_ref.1, s32[1,4,16]{2,1,0:T(4,128)} %halo_hbm.1, s32[1,4,8]{2,1,0:T(4,128)} %bitcast.4, f32[16,4096]{1,0:T(8,128)} %start_hbm.1, bf16[32,8,128,128]{3,2,1,0:T(8,128)(2,1)} %wts_ref.1), custom_call_target="tpu_custom_call" | custom-call | tf_op jit(solution)/shard_map/relax/pallas_call | solution.py:295
  35.8 0.0 copy-done.2
  35.9 0.0 copy-done
  35.9 0.0 copy-done.1
  35.9 6.9 %affinity.1 = (bf16[16,4096]{1,0:T(8,128)(2,1)}, bf16[32,8,128,128]{3,2,1,0:T(8,128)(2,1)}) custom-call(s32[8,32]{1,0:T(8,128)S(1)} %bitcast.3, s32[32]{0:T(128)S(1)} %copy-done.2, bf16[32,32,128]{2,1,0:T(8,128)(2,1)S(1)} %get-tuple-element.4.own_ref, bf16[128,32,128]{2,1,0:T(8,128)(2,1)S(1)} %get-tuple-element.5.table_ref, bf16[32,8,128,128]{3,2,1,0:T(8,128)(2,1)S(1)} %copy-done), custom_call_target="tpu_custom_call" | custom-call | tf_op jit(solution)/shard_map/affinity/pallas_call | solution.py:335
Async XLA Ops:
  0.6 35.2 %copy-start.2 = (s32[32]{0:T(128)S(1)}, s32[32]{0:T(128)}, u32[]{:S(2)}) copy-start(s32[32]{0:T(128)} %count_ref.1) | copy-start | bytes 388
  0.6 35.2 %copy-start = (bf16[32,8,128,128]{3,2,1,0:T(8,128)(2,1)S(1)}, bf16[32,8,128,128]{3,2,1,0:T(8,128)(2,1)}, u32[]{:S(2)}) copy-start(bf16[32,8,128,128]{3,2,1,0:T(8,128)(2,1)} %wts_ref.1) | copy-start | bytes 25165828
  0.7 35.2 %copy-start.1 = (s32[32,8]{0,1:T(8,128)S(1)}, s32[32,8]{0,1:T(8,128)}, u32[]{:S(2)}) copy-start(s32[32,8]{0,1:T(8,128)} %param.8) | copy-start | bytes 3076

commit v3 on v2

--- a/solution.py
+++ b/solution.py
@@ -163,7 +163,7 @@
                 return total
             return total + moved * moved
 
-        return lax.fori_loop(0, rows, one_row, total, unroll=8)
+        return lax.fori_loop(0, rows, one_row, total, unroll=16)
 
     for load in lists[1:]:
         load.wait()
@@ -260,25 +260,44 @@
         copy.wait_send()
 
 
-def affinity_kernel(cols_ref, count_ref, own_ref, table_ref, wts_ref, smoothed_ref, aff_ref):
-    per, slots, size = aff_ref.shape[:3]
+def affinity_kernel(
+    cols_ref, count_ref, own_ref, table_ref, wts_ref, smoothed_ref, aff_hbm, held, sem
+):
+    rows, slots, size = wts_ref.shape[:3]
     vecs = smoothed_ref.shape[0]
-    step = pl.program_id(0)
-
-    for i in range(per):
-        r = step * per + i
-        near = own_ref[r]
-        smoothed_ref[:, i * size : (i + 1) * size] = table_ref[r, 0:vecs]
-        far = jnp.concatenate([table_ref[cols_ref[s, r]] for s in range(slots)], axis=1)
-        below = lax.dot_general(
-            near, far, (((0,), (0,)), ((), ())), preferred_element_type=f32
-        )
-        for s in range(slots):
-            ratio = pl.reciprocal(below[:, s * size : (s + 1) * size], approx=True)
-            value = wts_ref[r, s].astype(f32) * ratio
-            if s >= MIN_LIVE:
-                value = jnp.where(s < count_ref[r], value, 0.0)
-            aff_ref[i, s] = value.astype(bf16)
+    chunks = sem.shape[0]
+    per = rows // chunks
+
+    def copy_out(c):
+        span = pl.ds(c * per, per)
+        return pltpu.make_async_copy(held.at[span], aff_hbm.at[span], sem.at[c])
+
+    def chunk(c, carry):
+        for i in range(per):
+            r = c * per + i
+            near = own_ref[r]
+            place = pl.ds(pl.multiple_of(r * size, size), size)
+            smoothed_ref[:, place] = table_ref[r, 0:vecs]
+            far = jnp.concatenate([table_ref[cols_ref[s, r]] for s in range(slots)], axis=1)
+            below = lax.dot_general(
+                near, far, (((0,), (0,)), ((), ())), preferred_element_type=f32
+            )
+            for s in range(slots):
+                ratio = pl.reciprocal(below[:, s * size : (s + 1) * size], approx=True)
+                value = wts_ref[r, s].astype(f32) * ratio
+                if s >= MIN_LIVE:
+                    value = jnp.where(s < count_ref[r], value, 0.0)
+                held[r, s] = value.astype(bf16)
+        copy_out(c).start()
+        return carry
+
+    [chunk(c, 0) for c in range(chunks)]
+
+    def finish(c, carry):
+        copy_out(c).wait()
+        return carry
+
+    lax.fori_loop(0, chunks, finish, 0)
 
 
 def local(n_region, n_sub, test_vectors, weights, block_cols, block_count, halo_send, far_send):
@@ -331,14 +350,13 @@
         name="relax",
     )(*[pltpu.with_memory_space_constraint(x, pltpu.HBM) for x in (cols, block_count, halo_send, far_lists, test_vectors, weights)])
 
-    per = 4
+    out_chunks = 16
     smoothed, affinity = pl.pallas_call(
         affinity_kernel,
         out_shape=(
             jax.ShapeDtypeStruct((vecs, rows * size), bf16),
             jax.ShapeDtypeStruct(weights.shape, bf16),
         ),
-        grid=(rows // per,),
         in_specs=[
             smem,
             smem,
@@ -347,9 +365,13 @@
             vmem,
         ],
         out_specs=(
-            pl.BlockSpec((vecs, per * size), lambda i: (0, i)),
-            pl.BlockSpec((per, slots, size, size), lambda i: (i, 0, 0, 0)),
-        ),
+            vmem,
+            pl.BlockSpec(memory_space=pltpu.HBM),
+        ),
+        scratch_shapes=[
+            pltpu.VMEM(weights.shape, bf16),
+            pltpu.SemaphoreType.DMA((out_chunks,)),
+        ],
         compiler_params=pltpu.CompilerParams(vmem_limit_bytes=32 * 1024 * 1024),
         name="affinity",
     )(cols, block_count, own_blocks, table_blocks, weights)

time: 43 us -> 40.3 us (0.937)
  Pallas kernels: 42.1 us -> 39.5 us
    pallas_call x1, Pallas kernels: 6.95 us -> 5 us  [local(): pl.pallas_call(affinity_kernel, out_shape=(jax.ShapeDtypeStruct((vecs, ro...]
    pallas_call x1, Pallas kernels: 35.2 us -> 34.5 us  [local(): pl.pallas_call(functools.partial(relax_kernel, n_region, n_sub), out_shap...]
where the time goes in v3:
time: 40.3 us; the launch traced here: 40.2 us
  Pallas kernels  39.5 us (98%)
  between operations  0.69 us (2%)
    pallas_call x1, Pallas kernels, local(): pl.pallas_call(functools.partial(relax_kernel, n_region, n_sub), out_shap...  34.5 us
    pallas_call x1, Pallas kernels, local(): pl.pallas_call(affinity_kernel, out_shape=(jax.ShapeDtypeStruct((vecs, ro...  5 us

profile of v3, /device:TPU:0, one launch (start us, length us, event | category | flops | bytes accessed | tf_op | source)
XLA Modules:
  0.0 40.2 jit_solution(13844790422990287353)
XLA Ops:
  0.6 0.0 copy-start.2
  0.6 0.0 copy-start
  0.7 0.0 copy-start.1
  0.7 34.5 %relax.1 = (bf16[32,32,128]{2,1,0:T(8,128)(2,1)S(1)}, bf16[128,32,128]{2,1,0:T(8,128)(2,1)S(1)}) custom-call(s32[8,32]{1,0:T(8,128)} %bitcast.2, s32[32]{0:T(128)} %count_ref.1, s32[1,4,16]{2,1,0:T(4,128)} %halo_hbm.1, s32[1,4,8]{2,1,0:T(4,128)} %bitcast.4, f32[16,4096]{1,0:T(8,128)} %start_hbm.1, bf16[32,8,128,128]{3,2,1,0:T(8,128)(2,1)} %wts_ref.1), custom_call_target="tpu_custom_call" | custom-call | tf_op jit(solution)/shard_map/relax/pallas_call | solution.py:314
  35.1 0.0 copy-done.2
  35.1 0.0 copy-done
  35.1 0.0 copy-done.1
  35.2 5.0 %affinity.1 = (bf16[16,4096]{1,0:T(8,128)(2,1)}, bf16[32,8,128,128]{3,2,1,0:T(8,128)(2,1)}) custom-call(s32[8,32]{1,0:T(8,128)S(1)} %bitcast.3, s32[32]{0:T(128)S(1)} %copy-done.2, bf16[32,32,128]{2,1,0:T(8,128)(2,1)S(1)} %get-tuple-element.4.own_ref, bf16[128,32,128]{2,1,0:T(8,128)(2,1)S(1)} %get-tuple-element.5.table_ref, bf16[32,8,128,128]{3,2,1,0:T(8,128)(2,1)S(1)} %copy-done), custom_call_target="tpu_custom_call" | custom-call | tf_op jit(solution)/shard_map/affinity/pallas_call | solution.py:354
Async XLA Ops:
  0.6 34.5 %copy-start.2 = (s32[32]{0:T(128)S(1)}, s32[32]{0:T(128)}, u32[]{:S(2)}) copy-start(s32[32]{0:T(128)} %count_ref.1) | copy-start | bytes 388
  0.6 34.5 %copy-start = (bf16[32,8,128,128]{3,2,1,0:T(8,128)(2,1)S(1)}, bf16[32,8,128,128]{3,2,1,0:T(8,128)(2,1)}, u32[]{:S(2)}) copy-start(bf16[32,8,128,128]{3,2,1,0:T(8,128)(2,1)} %wts_ref.1) | copy-start | bytes 25165828
  0.7 34.5 %copy-start.1 = (s32[32,8]{0,1:T(8,128)S(1)}, s32[32,8]{0,1:T(8,128)}, u32[]{:S(2)}) copy-start(s32[32,8]{0,1:T(8,128)} %param.8) | copy-start | bytes 3076
